TPU v7x, 32 devices: a whole 2x2x4 slice. The times are simulated.
32 devices in a mesh: dp: 8 (over z, x), perm: 2 (over y), blk: 2 (over core).
Axes of the slice: x: 2, y: 2, z: 4, core: 2. Of those that a mesh axis runs over, the one named last changes fastest.
Arguments:
- tokens: bfloat16 [16, 1024, 768], P('dp', 'blk'), may hold values from -6 to 6
- lengths: int32 [16], P('dp'), may hold values from 513 to 1024, as said below
- head_route: int32 [12], P('perm'), may hold values from 0 to 1, as said below
- w_query: bfloat16 [768, 768], P('blk', 'perm'), may hold values from -0.21875 to 0.21875
- b_query: bfloat16 [768], P(('perm', 'blk')), may hold values from -3 to 3
- w_key: bfloat16 [768, 768], P('blk', 'perm'), may hold values from -0.21875 to 0.21875
- w_value: bfloat16 [768, 768], P('blk', 'perm'), may hold values from -0.21875 to 0.21875
- b_value: bfloat16 [768], P(('perm', 'blk')), may hold values from -3 to 3
- w_out: bfloat16 [768, 768], P('perm', 'blk'), may hold values from -3.5 to 3.5
- b_out: bfloat16 [768], P('blk'), may hold values from -3 to 3
- first_gain: bfloat16 [768], P('blk'), may hold values from 0.25 to 1.75
- first_shift: bfloat16 [768], P('blk'), may hold values from -3 to 3
- w_inner: bfloat16 [768, 3072], P('blk', 'perm'), may hold values from -0.21875 to 0.21875
- b_inner: bfloat16 [3072], P(('perm', 'blk')), may hold values from -3 to 3
- w_outer: bfloat16 [3072, 768], P('perm', 'blk'), may hold values from -0.109375 to 0.109375
- b_outer: bfloat16 [768], P('blk'), may hold values from -3 to 3
- second_gain: bfloat16 [768], P('blk'), may hold values from 0.25 to 1.75
- second_shift: bfloat16 [768], P('blk'), may hold values from -3 to 3
- cotangent: bfloat16 [16, 1024, 768], P('dp', 'blk'), may hold values from -6 to 6
Outputs:
- layer_out: bfloat16 [16, 1024, 768], P('dp', 'blk')
- grad_tokens: bfloat16 [16, 1024, 768], P('dp', 'blk')
- grad_w_query: float32 [768, 768], P('blk', 'perm')
- grad_b_query: float32 [768], P(('perm', 'blk'))
- grad_w_key: float32 [768, 768], P('blk', 'perm')
- grad_w_value: float32 [768, 768], P('blk', 'perm')
- grad_b_value: float32 [768], P(('perm', 'blk'))
- grad_w_out: float32 [768, 768], P('perm', 'blk')
- grad_b_out: float32 [768], P('blk')
- grad_first_gain: float32 [768], P('blk')
- grad_first_shift: float32 [768], P('blk')
- grad_w_inner: float32 [768, 3072], P('blk', 'perm')
- grad_b_inner: float32 [3072], P(('perm', 'blk'))
- grad_w_outer: float32 [3072, 768], P('perm', 'blk')
- grad_b_outer: float32 [768], P('blk')
- grad_second_gain: float32 [768], P('blk')
- grad_second_shift: float32 [768], P('blk')
Inputs may be any that keep to these rules, and one draw needn't show every extreme that they name: `lengths`: every sequence holds more than 512 real tokens; in every draw some sequence is full. `head_route`: among the first 6 heads exactly half have 1, and likewise among the last 6.
All inputs are finite; a program needn't handle non-finite values.
Results may differ from a plain program's by a relative error of at most 0.018.
Values may be sent and summed in bfloat16 or wider, within the bound.
A program may use at most 192 MiB of HBM per device.

v0:
```python
from functools import partial
import math

import jax
import jax.numpy as jnp
from jax import lax
from jax.sharding import PartitionSpec as P

EPSILON = 1e-05
MASKED_SCORE = -1e30


def swapped_2(shard, axis, distance):
    return lax.ppermute(shard, axis, [(i, i ^ 1 << distance) for i in range(lax.axis_size(axis))])


def normalize(values, norm_gain, norm_shift):
    centre = values - jnp.mean(values, axis=-1, keepdims=True)
    spread = jnp.mean(centre * centre, axis=-1, keepdims=True)
    return centre * lax.rsqrt(spread + EPSILON) * norm_gain + norm_shift


def contract_rows(left_rows, right_rows):
    return lax.dot_general(
        left_rows, right_rows, (((0,), (0,)), ((), ())), preferred_element_type=jnp.float32
    )


def times_transposed(left_rows, weight_mat):
    return lax.dot_general(
        left_rows, weight_mat, (((1,), (1,)), ((), ())), preferred_element_type=jnp.float32
    )


def masked_scores(query_blocks, key_blocks, key_valid, score_scale):
    scores = (
        jnp.einsum("sqhe,skhe->shqk", query_blocks, key_blocks, preferred_element_type=jnp.float32)
        * score_scale
    )
    return jnp.where(key_valid[:, :, None, :], scores, MASKED_SCORE)


def column_sum(matrix):
    return jnp.sum(matrix.astype(jnp.float32), axis=0)


def per_device(
    tokens,
    lengths,
    head_route,
    w_query,
    b_query,
    w_key,
    w_value,
    b_value,
    w_out,
    b_out,
    first_gain,
    first_shift,
    w_inner,
    b_inner,
    w_outer,
    b_outer,
    second_gain,
    second_shift,
    cotangent,
):
    gathered = (
        lax.all_gather(w_query, "blk", axis=0, tiled=True),
        lax.all_gather(b_query, "blk", axis=0, tiled=True),
        lax.all_gather(w_key, "blk", axis=0, tiled=True),
        lax.all_gather(w_value, "blk", axis=0, tiled=True),
        lax.all_gather(b_value, "blk", axis=0, tiled=True),
        lax.all_gather(w_out, "blk", axis=1, tiled=True),
        lax.all_gather(b_out, "blk", axis=0, tiled=True),
        lax.all_gather(first_gain, "blk", axis=0, tiled=True),
        lax.all_gather(first_shift, "blk", axis=0, tiled=True),
        lax.all_gather(w_inner, "blk", axis=0, tiled=True),
        lax.all_gather(b_inner, "blk", axis=0, tiled=True),
        lax.all_gather(w_outer, "blk", axis=1, tiled=True),
        lax.all_gather(b_outer, "blk", axis=0, tiled=True),
        lax.all_gather(second_gain, "blk", axis=0, tiled=True),
        lax.all_gather(second_shift, "blk", axis=0, tiled=True),
    )
    (
        query_weight,
        query_bias,
        key_weight,
        value_weight,
        value_bias,
        out_weight,
        out_bias,
        gain_first,
        shift_first,
        inner_weight,
        inner_bias,
        outer_weight,
        outer_bias,
        gain_second,
        shift_second,
    ) = gathered
    gain_first = gain_first.astype(jnp.float32)
    shift_first = shift_first.astype(jnp.float32)
    gain_second = gain_second.astype(jnp.float32)
    shift_second = shift_second.astype(jnp.float32)
    seq_count, block_len, model_width = tokens.shape
    local_heads = head_route.shape[0]
    head_size = query_weight.shape[1] // local_heads
    swap_count = local_heads // 2
    score_scale = 1.0 / math.sqrt(head_size)
    total_rows = seq_count * block_len
    token_rows = tokens.reshape(total_rows, model_width)
    rows_float = token_rows.astype(jnp.float32)
    queries = (
        jnp.dot(token_rows, query_weight, preferred_element_type=jnp.float32)
        + query_bias.astype(jnp.float32)
    ).astype(jnp.bfloat16)
    key_rows = jnp.dot(token_rows, key_weight, preferred_element_type=jnp.float32).astype(
        jnp.bfloat16
    )
    value_rows = (
        jnp.dot(token_rows, value_weight, preferred_element_type=jnp.float32)
        + value_bias.astype(jnp.float32)
    ).astype(jnp.bfloat16)
    key_value = jnp.concatenate(
        [
            key_rows.reshape(total_rows, local_heads, head_size),
            value_rows.reshape(total_rows, local_heads, head_size),
        ],
        axis=2,
    )
    swap_heads = jnp.argsort(1 - head_route, stable=True)[:swap_count]
    picker = (swap_heads[:, None] == jnp.arange(local_heads)[None, :]).astype(jnp.bfloat16)
    outgoing = jnp.einsum(
        "rhc,gh->rgc", key_value, picker, preferred_element_type=jnp.float32
    ).astype(jnp.bfloat16)
    incoming = swapped_2(outgoing, "blk", 0)
    placed = jnp.einsum("rgc,gh->rhc", incoming, picker, preferred_element_type=jnp.float32).astype(
        jnp.bfloat16
    )
    swapped = (head_route == 1)[None, :, None]
    key_value_used = jnp.where(swapped, placed, key_value)
    head_shape = (seq_count, block_len, local_heads, head_size)
    query_blocks = queries.reshape(head_shape)
    key_blocks = key_value_used[:, :, :head_size].reshape(head_shape)
    value_blocks = key_value_used[:, :, head_size:].reshape(head_shape)
    block_index = lax.axis_index("blk")
    key_start = jnp.where(head_route == 1, (1 - block_index) * block_len, block_index * block_len)
    positions = key_start[:, None] + jnp.arange(block_len)[None, :]
    key_valid = positions[None] < lengths[:, None, None]
    scores = masked_scores(query_blocks, key_blocks, key_valid, score_scale)
    row_peak = jnp.max(scores, axis=-1, keepdims=True)
    raised = jnp.exp(scores - row_peak)
    row_total = jnp.sum(raised, axis=-1, keepdims=True)
    probabilities = raised / row_total
    log_total = row_peak + jnp.log(row_total)
    context = jnp.einsum(
        "shqk,skhe->sqhe",
        probabilities.astype(jnp.bfloat16),
        value_blocks,
        preferred_element_type=jnp.float32,
    ).astype(jnp.bfloat16)
    context = context.reshape(total_rows, local_heads * head_size)
    attended = lax.psum(
        jnp.dot(context, out_weight, preferred_element_type=jnp.float32), "perm"
    ) + out_bias.astype(jnp.float32)
    first_in = rows_float + attended
    first_out = normalize(first_in, gain_first, shift_first)
    first_low = first_out.astype(jnp.bfloat16)
    inner_pre = jnp.dot(
        first_low, inner_weight, preferred_element_type=jnp.float32
    ) + inner_bias.astype(jnp.float32)
    active = jax.nn.gelu(inner_pre, approximate=True)
    active_low = active.astype(jnp.bfloat16)
    outer_out = lax.psum(
        jnp.dot(active_low, outer_weight, preferred_element_type=jnp.float32).astype(jnp.bfloat16),
        "perm",
    ).astype(jnp.float32) + outer_bias.astype(jnp.float32)
    second_in = first_out + outer_out
    layer_out = (
        normalize(second_in, gain_second, shift_second).astype(jnp.bfloat16).reshape(tokens.shape)
    )
    upstream = cotangent.reshape(total_rows, model_width).astype(jnp.float32)
    unused_second, second_back = jax.vjp(normalize, second_in, gain_second, shift_second)
    grad_second_in, grad_second_gain, grad_second_shift = second_back(upstream)
    grad_outer = grad_second_in.astype(jnp.bfloat16)
    grad_b_outer = column_sum(grad_outer)
    grad_w_outer = contract_rows(active_low, grad_outer)
    grad_active = times_transposed(grad_outer, outer_weight)
    unused_gelu, gelu_back = jax.vjp(partial(jax.nn.gelu, approximate=True), inner_pre)
    grad_inner = gelu_back(grad_active)[0].astype(jnp.bfloat16)
    grad_b_inner = column_sum(grad_inner)
    grad_w_inner = contract_rows(first_low, grad_inner)
    grad_first = grad_second_in + lax.psum(
        times_transposed(grad_inner, inner_weight).astype(jnp.bfloat16), "perm"
    ).astype(jnp.float32)
    unused_first, first_back = jax.vjp(normalize, first_in, gain_first, shift_first)
    grad_first_in, grad_first_gain, grad_first_shift = first_back(grad_first)
    grad_attended = grad_first_in.astype(jnp.bfloat16)
    grad_b_out = column_sum(grad_attended)
    grad_w_out = contract_rows(context, grad_attended)
    grad_context = (
        times_transposed(grad_attended, out_weight).astype(jnp.bfloat16).reshape(head_shape)
    )
    scores = masked_scores(query_blocks, key_blocks, key_valid, score_scale)
    probabilities = jnp.exp(scores - log_total)
    grad_values = jnp.einsum(
        "shqk,sqhe->skhe",
        probabilities.astype(jnp.bfloat16),
        grad_context,
        preferred_element_type=jnp.float32,
    )
    grad_probabilities = jnp.einsum(
        "sqhe,skhe->shqk", grad_context, value_blocks, preferred_element_type=jnp.float32
    )
    inner_product = jnp.sum(probabilities * grad_probabilities, axis=-1, keepdims=True)
    grad_scores = (probabilities * (grad_probabilities - inner_product)).astype(jnp.bfloat16)
    grad_query_blocks = (
        jnp.einsum("shqk,skhe->sqhe", grad_scores, key_blocks, preferred_element_type=jnp.float32)
        * score_scale
    )
    grad_key_blocks = (
        jnp.einsum("shqk,sqhe->skhe", grad_scores, query_blocks, preferred_element_type=jnp.float32)
        * score_scale
    )
    grad_pairs = jnp.concatenate([grad_key_blocks, grad_values], axis=3).astype(jnp.bfloat16)
    grad_pairs = grad_pairs.reshape(total_rows, local_heads, 2 * head_size)
    returning = jnp.einsum(
        "rhc,gh->rgc", grad_pairs, picker, preferred_element_type=jnp.float32
    ).astype(jnp.bfloat16)
    arrived = swapped_2(returning, "blk", 0)
    arrived_placed = jnp.einsum(
        "rgc,gh->rhc", arrived, picker, preferred_element_type=jnp.float32
    ).astype(jnp.bfloat16)
    grad_own = jnp.where(swapped, arrived_placed, grad_pairs)
    grad_keys = grad_own[:, :, :head_size].reshape(total_rows, local_heads * head_size)
    grad_value_rows = grad_own[:, :, head_size:].reshape(total_rows, local_heads * head_size)
    grad_queries = grad_query_blocks.astype(jnp.bfloat16).reshape(
        total_rows, local_heads * head_size
    )
    grad_b_query = column_sum(grad_queries)
    grad_b_value = column_sum(grad_value_rows)
    grad_w_query = contract_rows(token_rows, grad_queries)
    grad_w_key = contract_rows(token_rows, grad_keys)
    grad_w_value = contract_rows(token_rows, grad_value_rows)
    back_terms = (
        times_transposed(grad_queries, query_weight)
        + times_transposed(grad_keys, key_weight)
        + times_transposed(grad_value_rows, value_weight)
    )
    grad_tokens = (
        grad_first_in + lax.psum(back_terms.astype(jnp.bfloat16), "perm").astype(jnp.float32)
    ).astype(jnp.bfloat16)
    grad_tokens = grad_tokens.reshape(tokens.shape)
    shares = (
        lax.psum_scatter(
            grad_w_query.astype(jnp.bfloat16), "blk", scatter_dimension=0, tiled=True
        ).astype(jnp.float32),
        lax.psum_scatter(
            grad_b_query.astype(jnp.bfloat16), "blk", scatter_dimension=0, tiled=True
        ).astype(jnp.float32),
        lax.psum_scatter(
            grad_w_key.astype(jnp.bfloat16), "blk", scatter_dimension=0, tiled=True
        ).astype(jnp.float32),
        lax.psum_scatter(
            grad_w_value.astype(jnp.bfloat16), "blk", scatter_dimension=0, tiled=True
        ).astype(jnp.float32),
        lax.psum_scatter(
            grad_b_value.astype(jnp.bfloat16), "blk", scatter_dimension=0, tiled=True
        ).astype(jnp.float32),
        lax.psum_scatter(
            grad_w_out.astype(jnp.bfloat16), "blk", scatter_dimension=1, tiled=True
        ).astype(jnp.float32),
        lax.psum_scatter(
            grad_b_out.astype(jnp.bfloat16), "blk", scatter_dimension=0, tiled=True
        ).astype(jnp.float32),
        lax.psum_scatter(
            grad_first_gain.astype(jnp.bfloat16), "blk", scatter_dimension=0, tiled=True
        ).astype(jnp.float32),
        lax.psum_scatter(
            grad_first_shift.astype(jnp.bfloat16), "blk", scatter_dimension=0, tiled=True
        ).astype(jnp.float32),
        lax.psum_scatter(
            grad_w_inner.astype(jnp.bfloat16), "blk", scatter_dimension=0, tiled=True
        ).astype(jnp.float32),
        lax.psum_scatter(
            grad_b_inner.astype(jnp.bfloat16), "blk", scatter_dimension=0, tiled=True
        ).astype(jnp.float32),
        lax.psum_scatter(
            grad_w_outer.astype(jnp.bfloat16), "blk", scatter_dimension=1, tiled=True
        ).astype(jnp.float32),
        lax.psum_scatter(
            grad_b_outer.astype(jnp.bfloat16), "blk", scatter_dimension=0, tiled=True
        ).astype(jnp.float32),
        lax.psum_scatter(
            grad_second_gain.astype(jnp.bfloat16), "blk", scatter_dimension=0, tiled=True
        ).astype(jnp.float32),
        lax.psum_scatter(
            grad_second_shift.astype(jnp.bfloat16), "blk", scatter_dimension=0, tiled=True
        ).astype(jnp.float32),
    )
    finals = lax.psum(
        (
            shares[0],
            shares[1],
            shares[2],
            shares[3],
            shares[4],
            shares[5],
            shares[6],
            shares[7],
            shares[8],
            shares[9],
            shares[10],
            shares[11],
            shares[12],
            shares[13],
            shares[14],
        ),
        "dp",
    )
    return (layer_out, grad_tokens) + tuple(finals)


def solution(mesh):
    placed = (
        P("dp", "blk", None),
        P("dp"),
        P("perm"),
        P("blk", "perm"),
        P(("perm", "blk")),
        P("blk", "perm"),
        P("blk", "perm"),
        P(("perm", "blk")),
        P("perm", "blk"),
        P("blk"),
        P("blk"),
        P("blk"),
        P("blk", "perm"),
        P(("perm", "blk")),
        P("perm", "blk"),
        P("blk"),
        P("blk"),
        P("blk"),
        P("dp", "blk", None),
    )
    return jax.shard_map(
        per_device,
        mesh=mesh,
        in_specs=placed,
        out_specs=(
            P("dp", "blk", None),
            P("dp", "blk", None),
            P("blk", "perm"),
            P(("perm", "blk")),
            P("blk", "perm"),
            P("blk", "perm"),
            P(("perm", "blk")),
            P("perm", "blk"),
            P("blk"),
            P("blk"),
            P("blk"),
            P("blk", "perm"),
            P(("perm", "blk")),
            P("perm", "blk"),
            P("blk"),
            P("blk"),
            P("blk"),
        ),
        check_vma=False,
    )
```

profile of v0, /device:TPU:0, one launch (start us, length us, event | category | flops | bytes accessed | tf_op | source)
XLA Modules:
  0.0 756.8 jit_solution(943402858456662586)
XLA Ops:
  44.4 4.2 bitcast_select_fusion.1
  55.1 4.9 fusion.13
  64.6 4.3 fusion.30
  82.3 79.6 %all-reduce.20.cloned.1.call-done = f32[1024,768]{1,0:T(8,128)} async-done(((f32[1024,768]{1,0:T(8,128)}), f32[1024,768]{1,0:T(8,128)}) %all-reduce.20.cloned.1.call-update) | async-done | bytes 3145744 | tf_op jit(solution)/shard_map/psum | solution.py:164
  165.4 6.6 fusion.56
  172.0 8.6 %convolution_convert_fusion.3 = bf16[1024,768]{1,0:T(8,128)(2,1)} fusion(bf16[1536,768]{1,0:T(8,128)(2,1)} %all-gather.12.cloned.1.call-done, f32[1024,1536]{1,0:T(8,128)} %fusion.56, f32[1536]{0:T(1024)S(1)} %reshape.222), kind=kOutput, calls=%fused_computation.51 | convolution fusion | flops 2432434176 | bytes 10229760 | tf_op jit(solution)/shard_map/dot_general | solution.py:176
  186.6 45.6 %all-reduce.22.cloned.1.call-done = bf16[1024,768]{1,0:T(8,128)(2,1)} async-done(((bf16[1024,768]{1,0:T(8,128)(2,1)}), bf16[1024,768]{1,0:T(8,128)(2,1)}) %all-reduce.22.cloned.1.call-update) | async-done | bytes 1572880 | tf_op jit(solution)/shard_map/psum | solution.py:175
  243.0 6.8 fusion.60
  251.6 3.7 convolution_convert_fusion.2
  255.5 51.4 %all-reduce.24.cloned.1.call-done = bf16[1024,768]{1,0:T(8,128)(2,1)} async-done(((bf16[1024,768]{1,0:T(8,128)(2,1)}), bf16[1024,768]{1,0:T(8,128)(2,1)}) %all-reduce.24.cloned.1.call-update) | async-done | bytes 1572880 | tf_op jit(solution)/shard_map/psum | solution.py:194
  306.9 3.7 multiply_reduce_fusion.1
  323.4 7.8 %fusion.25 = bf16[2,512,6,64]{1,3,2,0:T(8,128)(2,1)} fusion(f32[2,6,512]{2,1,0:T(8,128)S(1)} %log_add_fusion, f32[2,6,512,512]{2,3,1,0:T(8,128)} %copy-done, pred[2,6,512]{2,1,0:T(8,128)(4,1)S(1)} %broadcast_compare_fusion, bf16[2,512,6,64]{1,0,3,2:T(2,128)(2,1)} %reshape.193), kind=kOutput, calls=%fused_computation.68 | convolution fusion | flops 415629312 | bytes 14186496 | tf_op jit(solution)/shard_map/shqk,sqhe->skhe/dot_general | solution.py:207
  331.2 11.0 %multiply_reduce_fusion = (f32[2,6,512]{2,1,0:T(8,128)S(1)}, f32[2,6,512,512]{2,3,1,0:T(8,128)}) fusion(f32[2,6,512]{2,1,0:T(8,128)S(1)} %log_add_fusion, f32[2,6,512,512]{2,3,1,0:T(8,128)} %copy-done, pred[2,6,512]{2,1,0:T(8,128)(4,1)S(1)} %broadcast_compare_fusion, bf16[2,512,6,64]{1,3,2,0:T(8,128)(2,1)S(1)} %copy-done.14, ...), kind=kOutput, calls=%fused_computation.1 | convolution fusion | flops 418375680 | bytes 26793984 | tf_op jit(solution)/shard_map/sqhe,skhe->shqk/dot_general | solution.py:213
  344.5 10.1 %multiply_convert_fusion = bf16[2,6,512,512]{2,3,1,0:T(8,128)(2,1)S(1)} fusion(f32[2,6,512,512]{2,3,1,0:T(8,128)} %get-tuple-element.128, f32[2,6,512]{2,1,0:T(8,128)S(1)} %get-tuple-element.127, f32[2,6,512]{2,1,0:T(8,128)S(1)} %log_add_fusion, f32[2,6,512,512]{2,3,1,0:T(8,128)} %copy-done, pred[2,6,512]{2,1,0:T(8,128)(4,1)S(1)} %broadcast_compare_fusion), kind=kLoop, calls=%fused_computation | loop fusion | flops 18874368 | bytes 31512576 | tf_op jit(solution)/shard_map/convert_element_type | solution.py:217
  360.2 3.4 copy.101
  367.0 3.9 fusion.24
  379.0 4.8 bitcast_select_fusion
  383.8 3.5 slice_reduce_fusion
  410.6 8.8 %convolution_convert_fusion = bf16[1536,768]{1,0:T(8,128)(2,1)} fusion(bf16[1024,768]{1,0:T(8,128)(2,1)} %copy-done.27, f32[1024,1536]{1,0:T(8,128)} %fusion.56, f32[1536]{0:T(1024)S(1)} %reshape.222), kind=kOutput, calls=%fused_computation.28 | convolution fusion | flops 2432827392 | bytes 10229760 | tf_op jit(solution)/shard_map/dot_general | solution.py:24
  419.4 4.3 copy.121
  423.8 6.1 convolution_convert_fusion.1
  434.3 3.7 all-reduce.12
  445.2 16.9 %all-reduce.26.cloned.1.call-done = bf16[1024,768]{1,0:T(8,128)(2,1)} async-done(((bf16[1024,768]{1,0:T(8,128)(2,1)}), bf16[1024,768]{1,0:T(8,128)(2,1)}) %all-reduce.26.cloned.1.call-update) | async-done | bytes 1572880 | tf_op jit(solution)/shard_map/psum | solution.py:252
  466.9 279.1 %all-reduce.27 = (f32[384,384]{0,1:T(8,128)S(1)}, f32[192]{0:T(256)}, f32[384,384]{0,1:T(8,128)S(1)}, f32[384,384]{0,1:T(8,128)S(1)}, f32[192]{0:T(256)}, /*inde...) all-reduce(bf16[384,384]{0,1:T(8,128)(2,1)} %copy.114, ...), channel_id=1, replica_groups=mesh['dp'=8,'perm'=2,'blk'=2] {'dp'}, use_global_device_ids=true, to_apply=%region_17.18 | all-reduce | flops 1772928 | bytes 10644480 | tf_op jit(solution)/shard_map/psum | solution.py:302
  (246 shorter events, 154.4 us)
Async XLA Ops:
  8.0 154.0 %all-reduce.20.cloned.1.call-start = ((), (), s32[]{:S(2)}) async-start(), calls=%async_computation.6 | async-start | bytes 6291456 | tf_op jit(solution)/shard_map/psum | solution.py:164
  33.3 11.1 %collective-permute-start = (bf16[1024,3,128]{2,0,1:T(8,128)(2,1)}, bf16[1024,3,128]{2,0,1:T(8,128)(2,1)}, u32[]{:S(2)}, u32[]{:S(2)}) collective-permute-start(bf16[1024,3,128]{2,0,1:T(8,128)(2,1)} %copy.82), channel_id=1, source_target_pairs={{0,1},{1,0},{2,3},{3,2},{4,5},{5,4},{6,7},{7,6},{8,9},{9,8},{10,11... | collective-permute-start | bytes 2359304 | tf_op jit(solution)/shard_map/ppermute | solution.py:14
  44.2 25.7 %copy-start.25 = (bf16[384,768]{1,0:T(8,128)(2,1)}, bf16[384,768]{1,0:T(8,128)(2,1)S(1)}, u32[]{:S(2)}) copy-start(bf16[384,768]{1,0:T(8,128)(2,1)S(1)} %all_gather.50) | copy-start | bytes 1769476
  73.5 91.9 %all-gather.10.cloned.1.call-start = ((), (), s32[]{:S(2)}) async-start(), calls=%async_computation.7 | async-start | bytes 3538944 | tf_op jit(solution)/shard_map/all_gather | solution.py:78
  74.0 98.0 %all-gather.12.cloned.1.call-start = ((), (), s32[]{:S(2)}) async-start(), calls=%async_computation.8 | async-start | bytes 3538944 | tf_op jit(solution)/shard_map/all_gather | solution.py:80
  74.6 157.6 %all-reduce.22.cloned.1.call-start = ((), (), s32[]{:S(2)}) async-start(), calls=%async_computation.9 | async-start | bytes 3145728 | tf_op jit(solution)/shard_map/psum | solution.py:175
  172.0 8.7 %copy-start.35 = (bf16[384]{0:T(512)(128)(2,1)S(1)}, bf16[384]{0:T(512)(128)(2,1)}, u32[]{:S(2)}) copy-start(bf16[384]{0:T(512)(128)(2,1)} %param.34) | copy-start | bytes 2308
  172.0 10.5 %copy-start.36 = (bf16[384]{0:T(512)(128)(2,1)S(1)}, bf16[384]{0:T(512)(128)(2,1)}, u32[]{:S(2)}) copy-start(bf16[384]{0:T(512)(128)(2,1)} %param.35) | copy-start | bytes 2308
  172.0 12.4 %copy-start.37 = (bf16[384]{0:T(512)(128)(2,1)S(1)}, bf16[384]{0:T(512)(128)(2,1)}, u32[]{:S(2)}) copy-start(bf16[384]{0:T(512)(128)(2,1)} %param.36) | copy-start | bytes 2308
  180.6 126.3 %all-reduce.24.cloned.1.call-start = ((), (), s32[]{:S(2)}) async-start(), calls=%async_computation.10 | async-start | bytes 3145728 | tf_op jit(solution)/shard_map/psum | solution.py:194
  242.0 7.8 %copy-start.27 = (bf16[1024,768]{1,0:T(8,128)(2,1)}, bf16[1024,768]{1,0:T(8,128)(2,1)S(1)}, u32[]{:S(2)}) copy-start(bf16[1024,768]{1,0:T(8,128)(2,1)S(1)} %get-tuple-element.102) | copy-start | bytes 4718596
  243.0 8.5 %copy-start.40 = (bf16[768,1536]{1,0:T(8,128)(2,1)S(1)}, bf16[768,1536]{1,0:T(8,128)(2,1)}, u32[]{:S(2)}) copy-start(bf16[768,1536]{1,0:T(8,128)(2,1)} %all-gather.10.cloned.1.call-done) | copy-start | bytes 7077892
  255.3 183.1 %reduce-scatter.25.cloned.1.call-start = ((), (), s32[]{:S(2)}) async-start(), calls=%async_computation.16 | async-start | bytes 884736
  323.4 7.8 %copy-start.12 = (bf16[2,512,6,64]{1,0,3,2:T(2,128)(2,1)S(1)}, bf16[2,512,6,64]{1,0,3,2:T(2,128)(2,1)}, u32[]{:S(2)}) copy-start(bf16[2,512,6,64]{1,0,3,2:T(2,128)(2,1)} %reshape.193) | copy-start | bytes 2359300
  323.4 7.8 %copy-start.14 = (bf16[2,512,6,64]{1,3,2,0:T(8,128)(2,1)S(1)}, bf16[2,512,6,64]{1,3,2,0:T(8,128)(2,1)}, u32[]{:S(2)}) copy-start(bf16[2,512,6,64]{1,3,2,0:T(8,128)(2,1)} %copy.87) | copy-start | bytes 2359300
  344.3 95.3 %reduce-scatter.19.cloned.1.call-start = ((), (), s32[]{:S(2)}) async-start(), calls=%async_computation.13 | async-start | bytes 884736
  344.5 12.7 %copy-start.10 = (bf16[2,512,6,64]{1,0,3,2:T(2,128)(2,1)S(1)}, bf16[2,512,6,64]{1,0,3,2:T(2,128)(2,1)}, u32[]{:S(2)}) copy-start(bf16[2,512,6,64]{1,0,3,2:T(2,128)(2,1)} %reshape.189) | copy-start | bytes 2359300
  371.9 7.1 collective-permute-start.1
  378.7 62.7 %reduce-scatter.23.cloned.1.call-start = ((), (), s32[]{:S(2)}) async-start(), calls=%async_computation.15 | async-start | bytes 884736
  395.8 47.5 %reduce-scatter.21.cloned.1.call-start = ((), (), s32[]{:S(2)}) async-start(), calls=%async_computation.14 | async-start | bytes 884736
  404.3 57.9 %all-reduce.26.cloned.1.call-start = ((), (), s32[]{:S(2)}) async-start(), calls=%async_computation.11 | async-start | bytes 3145728 | tf_op jit(solution)/shard_map/psum | solution.py:252
  410.3 54.8 %reduce-scatter.27.cloned.1.call-start = ((), (), s32[]{:S(2)}) async-start(), calls=%async_computation.17 | async-start | bytes 3538944
  423.7 43.2 %reduce-scatter.17.cloned.1.call-start = ((), (), s32[]{:S(2)}) async-start(), calls=%async_computation.12 | async-start | bytes 3538944 | tf_op jit(solution)/shard_map/reduce_scatter | solution.py:283
  429.8 32.3 %copy-start.6 = (f32[1024,768]{1,0:T(8,128)S(1)}, f32[1024,768]{1,0:T(8,128)}, u32[]{:S(2)}) copy-start(f32[1024,768]{1,0:T(8,128)} %copy-done.5) | copy-start | bytes 9437188
  (35 other events, 122.6 us)
Sparse Core Ops, SparseCore 0:
  73.6 88.3 all-reduce.19
  180.7 51.4 all-reduce.21
  255.4 51.4 all-reduce.23
  410.4 51.7 all-reduce.25
Sparse Core Ops, SparseCore 1:
  75.5 13.4 all-gather.9
  90.5 11.9 all-gather.11
  344.4 7.9 reduce-scatter.24
  378.8 8.0 reduce-scatter.18
  395.8 8.0 reduce-scatter.22
  406.3 9.1 reduce-scatter.20
  423.8 9.9 reduce-scatter.26
  436.5 11.0 reduce-scatter.16
where the time goes:
time: 764 us; the launch traced here: 757 us
  blocking collectives  308 us (40%)
  waiting for transfers between devices  195 us (26%)
  matrix products  115 us (15%)
  local copies, waits for them, and re-layouts  77.4 us (10%)
  other arithmetic  39.4 us (5%)
  between operations  19.6 us (3%)
    psum x1, blocking collectives, per_device(): lax.psum((shares[0], shares[1], shares[2], shares[3], shares[4], shares[5...  279 us
    psum x1, waiting for transfers between devices, per_device(): lax.psum(jnp.dot(context, out_weight, preferred_element_type=jnp.float32)...  79.6 us
    psum x1, waiting for transfers between devices, per_device(): lax.psum(times_transposed(grad_inner, inner_weight).astype(jnp.bfloat16),...  51.4 us
    psum x1, waiting for transfers between devices, per_device(): lax.psum(jnp.dot(active_low, outer_weight, preferred_element_type=jnp.flo...  45.6 us
    unnamed x117, local copies, waits for them, and re-layouts  41.5 us
    dot_general x6, matrix products, contract_rows(): lax.dot_general(left_rows, right_rows, (((0,), (0,)), ((), ())), preferre...  24.6 us
    dot_general x6, matrix products, times_transposed(): lax.dot_general(left_rows, weight_mat, (((1,), (1,)), ((), ())), preferre...  18 us
    psum x1, waiting for transfers between devices, per_device(): lax.psum(back_terms.astype(jnp.bfloat16), 'perm').astype(jnp.float32)  16.9 us
  transfers between devices with their start and end apart: 14, of which 4 were waited for; matrix products, arithmetic and copies ran while one was open for 14% of the time, Pallas kernels for 0%

commit v1 on v0

v1 whole, which is shorter than its diff:
```python
import functools
import math

import jax
import jax.numpy as jnp
from jax import lax
from jax.experimental import pallas as pl
from jax.experimental.pallas import tpu as pltpu
from jax.sharding import PartitionSpec as P

EPSILON = 1e-05
MASKED_SCORE = -1e30
MESH = pl.DeviceIdType.MESH
F32 = jnp.float32
BF16 = jnp.bfloat16
GELU_C = math.sqrt(2.0 / math.pi)


def nn(left, right):
    return lax.dot_general(left, right, (((1,), (0,)), ((), ())), preferred_element_type=F32)


def nt(left, right):
    return lax.dot_general(left, right, (((1,), (1,)), ((), ())), preferred_element_type=F32)


def al(value, multiple):
    return pl.multiple_of(value, multiple)


R_BQ, R_BV, R_BO, R_G1, R_S1, R_B2, R_G2, R_S2, R_B1, R_LANE, R_HEAD = 0, 1, 2, 3, 4, 5, 6, 7, 8, 12, 16


def layer_kernel(
    heads,
    tokens, cot, lengths, vec, wq, wk, wv, wo, w1, w2,
    layer_out, grad_tokens, gk, gs, gv,
    xo, xx, cotb, gwq, gwk, gwv, gwo, gw1, gw2, vecs, vecf, biasb,
    q, k, v, c, flow, xh1, rs1, lse, act, dact, acc, go, tA, tB, dc, dq, dk, dv, lob, wide, backs, backr, hrow, b1r, gb1,
    sem_l, sem_s, sem_r,
):
    d, p, b = lax.axis_index("dp"), lax.axis_index("perm"), lax.axis_index("blk")
    D = xo.shape[1]
    L = xo.shape[0]
    FF = gw2.shape[0]
    DH, FH = D // 2, FF // 2
    NP = heads // 4
    xbit = lax.rem(d, 2)
    core, ypeer, diag = (d, p, 1 - b), (d, 1 - p, b), (d, 1 - p, 1 - b)
    xpeer = (d + 1 - 2 * xbit, p, b)

    bar = pltpu.get_barrier_semaphore()
    peers = (core, ypeer, diag, xpeer)
    for peer in peers:
        pl.semaphore_signal(bar, 1, device_id=peer, device_id_type=MESH)
    pl.semaphore_wait(bar, len(peers))

    count = [0]
    sent = []

    def rc(src, dst, peer):
        i = count[0]
        count[0] += 1
        cp = pltpu.make_async_remote_copy(
            src_ref=src, dst_ref=dst, send_sem=sem_s.at[i], recv_sem=sem_r.at[i],
            device_id=peer, device_id_type=MESH)
        cp.start()
        sent.append(cp)
        return cp

    nl = [0]

    def lc(src, dst):
        i = nl[0]
        nl[0] += 1
        cp = pltpu.make_async_copy(src, dst, sem_l.at[i])
        cp.start()
        return cp

    shards = (wq, wk, wv, wo, w1, w2)
    full = (gwq, gwk, gwv, gwo, gw1, gw2)
    rows_by_blk = (True, True, True, False, True, False)

    def place(n, pp, bb):
        sr, sc = shards[n].shape
        if rows_by_blk[n]:
            return bb * sr, pp * sc, sr, sc
        return pp * sr, bb * sc, sr, sc

    def region(n, pp, bb):
        r0, c0, sr, sc = place(n, pp, bb)
        return full[n].at[pl.ds(al(r0, 128), sr), pl.ds(al(c0, 128), sc)]

    def region_half(n, pp, bb, xh):
        r0, c0, sr, sc = place(n, pp, bb)
        return full[n].at[pl.ds(al(r0 + xh * (sr // 2), 64), sr // 2), pl.ds(al(c0, 128), sc)]

    vecs[0] = vec[...]
    cp_x = lc(tokens.at[p], xo)
    own = [lc(shards[n], region(n, p, b)) for n in range(6)]
    cp_cot = lc(cot.at[p], cotb)
    v_c = rc(vecs.at[0], vecs.at[1], core)
    v_y = rc(vecs.at[0], vecs.at[2], ypeer)
    v_d = rc(vecs.at[0], vecs.at[3], diag)
    x_c = rc(tokens.at[p], xx, core)
    to_core = []
    to_y = []
    for n in range(6):
        sr = shards[n].shape[0]
        to_core.append(rc(shards[n], region(n, p, b), core))
        to_y.append(rc(shards[n].at[pl.ds(al(xbit * (sr // 2), 64), sr // 2)], region_half(n, p, b, xbit), ypeer))
    to_x = [None] * 6
    to_c1 = [None] * 6
    to_c2 = [None] * 6

    def svc1(n):
        to_y[n].wait_recv()
        src = region_half(n, 1 - p, b, xbit)
        to_x[n] = rc(src, src, xpeer)
        to_c1[n] = rc(src, src, core)

    def svc2(n):
        to_x[n].wait_recv()
        src = region_half(n, 1 - p, b, 1 - xbit)
        to_c2[n] = rc(src, src, core)

    def need(n):
        to_c1[n].wait_recv()
        to_c2[n].wait_recv()

    cp_x.wait()
    for cp in (v_c, v_y, v_d):
        cp.wait_recv()
    vecf[...] = (vecs[0] + vecs[1]) + (vecs[2] + vecs[3])
    for head in range(heads):
        hrow[head] = vecf[R_HEAD + head:R_HEAD + head + 1, 0:128]
    for t in range(FF // D):
        b1r[t] = vecf[R_B1 + t:R_B1 + t + 1, :]
    length = lengths[p]
    pos = lax.broadcasted_iota(jnp.int32, (L, 128), 0)
    for which in range(2):
        start = (b if which == 0 else 1 - b) * L
        biasb[which] = jnp.where(pos + start < length, 0.0, MASKED_SCORE)
    x_c.wait_recv()

    lane = lax.broadcasted_iota(jnp.int32, (1, 128), 1)

    def head_lanes(hh):
        return (lane < 64) if hh == 0 else (lane >= 64)

    def head_bias(head):
        return jnp.where(hrow[head] > 0.5, biasb[1], biasb[0])

    def project(h):
        cols = pl.ds(al(h * DH, 128), DH)
        swapped = vecf[R_LANE:R_LANE + 1, cols] > 0.5
        q[:, cols] = (nn(xo[...], gwq[:, cols]) + vecf[R_BQ:R_BQ + 1, cols]).astype(BF16) * jnp.asarray(0.125, BF16)
        k[:, cols] = jnp.where(swapped, nn(xx[...], gwk[:, cols]), nn(xo[...], gwk[:, cols])).astype(BF16)
        v[:, cols] = (jnp.where(swapped, nn(xx[...], gwv[:, cols]), nn(xo[...], gwv[:, cols]))
                      + vecf[R_BV:R_BV + 1, cols]).astype(BF16)

    def attend(h, j):
        cols = pl.ds(al(h * DH + j * 128, 128), 128)
        kp, vp = k[:, cols], v[:, cols]
        vT = vp.T
        tops = []
        for hh in range(2):
            head = h * (heads // 2) + 2 * j + hh
            km = jnp.where(head_lanes(hh), kp, jnp.zeros_like(kp))
            bias = head_bias(head)
            bias = jnp.concatenate([bias, bias], axis=1)
            parts = []
            for t in range(L // 256):
                s = nt(km, q[t * 256:(t + 1) * 256, cols]) + bias
                peak = jnp.max(s, axis=0, keepdims=True)
                e = jnp.exp(s - peak)
                total = jnp.sum(e, axis=0, keepdims=True)
                lse[head, :, t * 256:(t + 1) * 256] = peak + jnp.log(total)
                parts.append(nn(vT[hh * 64:(hh + 1) * 64, :], e.astype(BF16)) * (1.0 / total))
            tops.append(jnp.concatenate(parts, axis=1))
        c[:, cols] = jnp.concatenate(tops, axis=0).T.astype(BF16)

    for n in range(4):
        own[n].wait()
        to_core[n].wait_recv()
    project(p)
    svc1(0)
    svc1(1)

    def own_pair(j, carry):
        attend(p, j)
        return carry

    lax.fori_loop(0, NP, own_pair, 0)
    svc1(2)
    svc1(3)
    for n in range(4):
        svc2(n)
    for n in range(4):
        need(n)
    project(1 - p)

    def other_pair(j, carry):
        attend(1 - p, j)
        return carry

    lax.fori_loop(0, NP, other_pair, 0)
    svc1(4)
    svc1(5)

    acc[...] = nn(c[...], gwo[...])
    TR = 128

    def rows_of(i):
        return pl.ds(al(i * TR, TR), TR)

    def norm1(i, carry):
        r = rows_of(i)
        val = xo[r, :].astype(F32) + (acc[r, :] + vecf[R_BO:R_BO + 1, :])
        centre = val - jnp.mean(val, axis=1, keepdims=True)
        spread = jnp.mean(centre * centre, axis=1, keepdims=True)
        rs = lax.rsqrt(spread + EPSILON)
        xh = centre * rs
        xh1[r, :] = xh
        rs1[r, :] = jnp.broadcast_to(rs, (TR, 128))
        flow[r, :] = (xh * vecf[R_G1:R_G1 + 1, :] + vecf[R_S1:R_S1 + 1, :]).astype(BF16)
        return carry

    lax.fori_loop(0, L // TR, norm1, 0)
    tA[...] = flow[...].T

    NT = FH // D

    def ff_tile(h, i, first):
        hid = pl.ds(al(h * FH + i * D, 128), D)
        wide[...] = nn(flow[...], gw1[:, hid])

        def gelu_rows(j, carry):
            r = pl.ds(al(j * 32, 32), 32)
            u = wide[r, :] + b1r[h * NT + i]
            uu = u * u
            th = jnp.tanh(GELU_C * u * (1.0 + 0.044715 * uu))
            half = 0.5 * (1.0 + th)
            act[r, hid] = (u * half).astype(BF16)
            slope = half + 0.5 * u * (1.0 - th * th) * (GELU_C * (1.0 + 3 * 0.044715 * uu))
            dact[r, hid] = slope.astype(BF16)
            return carry

        lax.fori_loop(0, L // 32, gelu_rows, 0)
        out = nn(act[:, hid], gw2[hid, :])
        if first:
            acc[...] = out
        else:
            acc[...] += out

    for n in (4, 5):
        own[n].wait()
        to_core[n].wait_recv()
    ff_tile(p, 0, True)
    for i in range(1, NT):
        ff_tile(p, i, False)
    svc2(4)
    svc2(5)
    need(4)
    need(5)

    def ff_other(i, carry):
        ff_tile(1 - p, i, False)
        return carry

    lax.fori_loop(0, NT, ff_other, 0)

    cp_cot.wait()
    zero = jnp.zeros((1, D), F32)
    for r0 in range(gv.shape[0]):
        gv[r0:r0 + 1, :] = zero

    def colsum(x):
        return jnp.sum(x, axis=0, keepdims=True)

    def norm2(i, carry):
        dg, ds, db = carry
        r = rows_of(i)
        fo = xh1[r, :] * vecf[R_G1:R_G1 + 1, :] + vecf[R_S1:R_S1 + 1, :]
        val = fo + (acc[r, :] + vecf[R_B2:R_B2 + 1, :])
        centre = val - jnp.mean(val, axis=1, keepdims=True)
        spread = jnp.mean(centre * centre, axis=1, keepdims=True)
        rs = lax.rsqrt(spread + EPSILON)
        xh = centre * rs
        g2 = vecf[R_G2:R_G2 + 1, :]
        lob[r, :] = (xh * g2 + vecf[R_S2:R_S2 + 1, :]).astype(BF16)
        up = cotb[r, :].astype(F32)
        dxh = up * g2
        gin = rs * (dxh - jnp.mean(dxh, axis=1, keepdims=True) - xh * jnp.mean(dxh * xh, axis=1, keepdims=True))
        acc[r, :] = gin
        low = gin.astype(BF16)
        go[r, :] = low
        return dg + colsum(up * xh), ds + colsum(up), db + colsum(low.astype(F32))

    dg, ds, db = lax.fori_loop(0, L // TR, norm2, (zero, zero, zero))
    gv[R_G2:R_G2 + 1, :] = dg
    gv[R_S2:R_S2 + 1, :] = ds
    gv[R_B2:R_B2 + 1, :] = db
    lo_local = lc(lob, layer_out.at[p])
    lo_y = rc(lob, layer_out.at[p], ypeer)

    tB[...] = go[...].T
    keep_rows = pl.ds(al(b * DH, 128), DH)
    send_rows = pl.ds(al((1 - b) * DH, 128), DH)

    def weight_grad(leftT, right, h, col, width):
        at = pl.ds(al(col, 128), width)
        gs[h, :, at] = nn(leftT[send_rows, :], right).astype(BF16)
        gk[h, :, at] = nn(leftT[keep_rows, :], right).astype(BF16)

    def ff_back(h, i):
        hid = pl.ds(al(h * FH + i * D, 128), D)
        du = (nt(go[...], gw2[hid, :]) * dact[:, hid].astype(F32)).astype(BF16)
        gb1[h * NT + i] = colsum(du.astype(F32))
        dact[:, hid] = du
        acc[...] += nt(dact[:, hid], gw1[:, hid])
        weight_grad(tA, dact[:, hid], h, i * D, D)
        weight_grad(tB, act[:, hid], h, FH + i * D, D)

    def ff_back_own(i, carry):
        ff_back(p, i)
        return carry

    def ff_back_other(i, carry):
        ff_back(1 - p, i)
        return carry

    lax.fori_loop(0, NT, ff_back_other, 0)
    lax.fori_loop(0, NT, ff_back_own, 0)

    for t in range(FF // D):
        gv[R_B1 + t:R_B1 + t + 1, :] = gb1[t]

    def norm1_back(i, carry):
        dg, ds, db = carry
        r = rows_of(i)
        up = acc[r, :]
        xh = xh1[r, :]
        dxh = up * vecf[R_G1:R_G1 + 1, :]
        gin = rs1[r, 0:1] * (dxh - jnp.mean(dxh, axis=1, keepdims=True) - xh * jnp.mean(dxh * xh, axis=1, keepdims=True))
        acc[r, :] = gin
        low = gin.astype(BF16)
        go[r, :] = low
        return dg + colsum(up * xh), ds + colsum(up), db + colsum(low.astype(F32))

    dg, ds, db = lax.fori_loop(0, L // TR, norm1_back, (zero, zero, zero))
    gv[R_G1:R_G1 + 1, :] = dg
    gv[R_S1:R_S1 + 1, :] = ds
    gv[R_BO:R_BO + 1, :] = db
    tB[...] = go[...].T
    dc[...] = nt(go[...], gwo[...]).astype(BF16)
    for h in range(2):
        weight_grad(tB, c[:, h * DH:(h + 1) * DH], h, 2 * FH, DH)
    tA[...] = xo[...].T
    tB[...] = xx[...].T

    def attend_back(j, carry):
        cols = pl.ds(al(j * 128, 128), 128)
        kp, vp, qp, dcp = k[:, cols], v[:, cols], q[:, cols], dc[:, cols]
        kT = kp.T
        dkv = [jnp.zeros((L, 128), F32), jnp.zeros((L, 128), F32)]
        tops = []
        for hh in range(2):
            head = 2 * j + hh
            mine = head_lanes(hh)
            none = jnp.zeros_like(kp)
            km, vm = jnp.where(mine, kp, none), jnp.where(mine, vp, none)
            qm, dcm = jnp.where(mine, qp, none), jnp.where(mine, dcp, none)
            bias = head_bias(head)
            bias = jnp.concatenate([bias, bias], axis=1)
            parts = []
            for t in range(L // 256):
                ts = slice(t * 256, (t + 1) * 256)
                prob = jnp.exp(nt(km, qp[ts]) + bias - lse[head, :, ts])
                dprob = nt(vm, dcp[ts])
                delta = jnp.sum(prob * dprob, axis=0, keepdims=True)
                dscore = (prob * (dprob - delta)).astype(BF16)
                dkv[1] += nn(prob.astype(BF16), dcm[ts])
                dkv[0] += nn(dscore, qm[ts])
                parts.append(nn(kT[hh * 64:(hh + 1) * 64, :], dscore))
            tops.append(jnp.concatenate(parts, axis=1))
        dq[:, cols] = (jnp.concatenate(tops, axis=0).T * 0.125).astype(BF16)
        dk[:, cols] = dkv[0].astype(BF16)
        dv[:, cols] = dkv[1].astype(BF16)
        return carry

    lax.fori_loop(0, 2 * NP, attend_back, 0)
    gv[R_BQ:R_BQ + 1, :] = colsum(dq[...].astype(F32))
    gv[R_BV:R_BV + 1, :] = colsum(dv[...].astype(F32))

    swapped = vecf[R_LANE:R_LANE + 1, :] > 0.5
    none = jnp.zeros((L, D), BF16)
    dc[...] = jnp.where(swapped, dk[...], none)
    flow[...] = jnp.where(swapped, dv[...], none)
    dk[...] = jnp.where(swapped, none, dk[...])
    dv[...] = jnp.where(swapped, none, dv[...])
    backs[...] = (nt(dc[...], gwk[...]) + nt(flow[...], gwv[...])).astype(BF16)
    back_c = rc(backs, backr, core)
    for h in range(2):
        hs = slice(h * DH, (h + 1) * DH)
        for n, (a, x) in enumerate(((dq, None), (dk, dc), (dv, flow))):
            at = slice(2 * FH + DH + n * DH, 2 * FH + 2 * DH + n * DH)
            for dst, rows in ((gs, send_rows), (gk, keep_rows)):
                val = nn(tA[rows, :], a[:, hs])
                if x is not None:
                    val = val + nn(tB[rows, :], x[:, hs])
                dst[h, :, at] = val.astype(BF16)
    acc[...] += nt(dq[...], gwq[...]) + nt(dk[...], gwk[...]) + nt(dv[...], gwv[...])
    lo_local.wait()
    lo_y.wait_send()
    back_c.wait_recv()
    lob[...] = (acc[...] + backr[...].astype(F32)).astype(BF16)
    gt_local = lc(lob, grad_tokens.at[p])
    gt_y = rc(lob, grad_tokens.at[p], ypeer)
    gt_local.wait()
    gt_y.wait_recv()
    lo_y.wait_recv()
    for cp in sent:
        if cp is not lo_y:
            cp.wait_send()


def per_device(
    tokens, lengths, head_route, w_query, b_query, w_key, w_value, b_value, w_out, b_out,
    first_gain, first_shift, w_inner, b_inner, w_outer, b_outer, second_gain, second_shift, cotangent,
):
    p, b = lax.axis_index("perm"), lax.axis_index("blk")
    L, D = tokens.shape[1:]
    FF = w_inner.shape[1] * 2
    heads = head_route.shape[0] * 2
    hd = D // heads
    quarter = p * 2 + b

    def put(vector, offset, keep=None):
        vector = vector.astype(F32)
        if keep is not None:
            vector = jnp.where(keep, vector, 0.0)
        return lax.dynamic_update_slice(jnp.zeros((D,), F32), vector, (offset,))

    first_p, first_b = p == 0, b == 0
    by_blk = b * (D // 2)
    route = head_route.astype(F32)
    rows = [put(b_query, quarter * (D // 4)), put(b_value, quarter * (D // 4))]
    rows += [put(a, by_blk, first_p) for a in (b_out, first_gain, first_shift, b_outer, second_gain, second_shift)]
    hidden = lax.dynamic_update_slice(jnp.zeros((FF,), F32), b_inner.astype(F32), (quarter * (FF // 4),)).reshape(FF // D, D)
    lane_route = put(jnp.repeat(route, hd), p * (D // 2), first_b)
    head_rows = lax.dynamic_update_slice(
        jnp.zeros((16, D), F32),
        jnp.broadcast_to(jnp.where(first_b, route, 0.0)[:, None], (heads // 2, D)),
        (p * (heads // 2), 0))
    vec = jnp.concatenate([jnp.stack(rows), hidden, lane_route[None], jnp.zeros((3, D), F32), head_rows], axis=0)

    half = FF + 4 * (D // 2)
    any_ = pl.BlockSpec(memory_space=pl.ANY)
    vm = pl.BlockSpec(memory_space=pltpu.VMEM)
    V = pltpu.VMEM
    layer_out, grad_tokens, gk, gs, gv = pl.pallas_call(
        functools.partial(layer_kernel, heads),
        out_shape=(
            jax.ShapeDtypeStruct(tokens.shape, BF16),
            jax.ShapeDtypeStruct(tokens.shape, BF16),
            jax.ShapeDtypeStruct((2, D // 2, half), BF16),
            jax.ShapeDtypeStruct((2, D // 2, half), BF16),
            jax.ShapeDtypeStruct((16, D), F32),
        ),
        in_specs=[any_, any_, pl.BlockSpec(memory_space=pltpu.SMEM), vm] + [any_] * 6,
        out_specs=(any_, any_, vm, vm, vm),
        scratch_shapes=[
            V((L, D), BF16), V((L, D), BF16), V((L, D), BF16),
            V((D, D), BF16), V((D, D), BF16), V((D, D), BF16), V((D, D), BF16), V((D, FF), BF16), V((FF, D), BF16),
            V((4, 32, D), F32), V((32, D), F32), V((2, L, 128), F32),
            V((L, D), BF16), V((L, D), BF16), V((L, D), BF16), V((L, D), BF16),
            V((L, D), BF16), V((L, D), F32), V((L, 128), F32), V((16, 1, L), F32),
            V((L, FF), BF16), V((L, FF), BF16), V((L, D), F32), V((L, D), BF16),
            V((D, L), BF16), V((D, L), BF16), V((L, D), BF16),
            V((L, D), BF16), V((L, D), BF16), V((L, D), BF16), V((L, D), BF16),
            V((L, D), F32), V((L, D), BF16), V((L, D), BF16),
            V((16, 1, 128), F32), V((FF // D, 1, D), F32), V((FF // D, 1, D), F32),
            pltpu.SemaphoreType.DMA((16,)),
            pltpu.SemaphoreType.DMA((48,)),
            pltpu.SemaphoreType.DMA((48,)),
        ],
        compiler_params=pltpu.CompilerParams(collective_id=0, has_side_effects=True, vmem_limit_bytes=62 * 2**20),
        name="layer",
    )(tokens, cotangent, lengths, vec, w_query, w_key, w_value, w_out, w_inner, w_outer)

    share = gk.astype(F32) + lax.ppermute(gs, "blk", [(0, 1), (1, 0)]).astype(F32)
    other = lax.dynamic_index_in_dim(share, 1 - p, 0, keepdims=False).astype(BF16)
    mine = lax.dynamic_index_in_dim(share, p, 0, keepdims=False)
    mine = mine + lax.ppermute(other, "perm", [(0, 1), (1, 0)]).astype(F32)
    mine = lax.psum(mine.astype(BF16), "dp").astype(F32)
    vectors = lax.psum(gv, ("dp", "perm", "blk"))

    DH, FH = D // 2, FF // 2
    at = 2 * FH

    def of_blk(row):
        return lax.dynamic_slice(vectors[row], (b * DH,), (DH,))

    def of_quarter(row):
        return lax.dynamic_slice(vectors[row], (quarter * (D // 4),), (D // 4,))

    hidden_grad = lax.dynamic_slice(vectors[R_B1:R_B1 + FF // D].reshape(FF), (quarter * (FF // 4),), (FF // 4,))
    return (
        layer_out,
        grad_tokens,
        mine[:, at + DH:at + 2 * DH],
        of_quarter(R_BQ),
        mine[:, at + 2 * DH:at + 3 * DH],
        mine[:, at + 3 * DH:at + 4 * DH],
        of_quarter(R_BV),
        mine[:, at:at + DH].T,
        of_blk(R_BO),
        of_blk(R_G1),
        of_blk(R_S1),
        mine[:, :FH],
        hidden_grad,
        mine[:, FH:at].T,
        of_blk(R_B2),
        of_blk(R_G2),
        of_blk(R_S2),
    )


def solution(mesh):
    placed = (
        P("dp", "blk", None), P("dp"), P("perm"), P("blk", "perm"), P(("perm", "blk")), P("blk", "perm"),
        P("blk", "perm"), P(("perm", "blk")), P("perm", "blk"), P("blk"), P("blk"), P("blk"), P("blk", "perm"),
        P(("perm", "blk")), P("perm", "blk"), P("blk"), P("blk"), P("blk"), P("dp", "blk", None),
    )
    outs = (
        P("dp", "blk", None), P("dp", "blk", None), P("blk", "perm"), P(("perm", "blk")), P("blk", "perm"),
        P("blk", "perm"), P(("perm", "blk")), P("perm", "blk"), P("blk"), P("blk"), P("blk"), P("blk", "perm"),
        P(("perm", "blk")), P("perm", "blk"), P("blk"), P("blk"), P("blk"),
    )
    return jax.shard_map(per_device, mesh=mesh, in_specs=placed, out_specs=outs, check_vma=False)
```

time: 764 us -> 429 us (0.56)
  blocking collectives: 308 us -> 43.2 us
  Pallas kernels: 0 us -> 135 us
  matrix products: 115 us -> 0 us
  local copies, waits for them, and re-layouts: 77.4 us -> 23.1 us
  waiting for transfers between devices: 195 us -> 183 us
  other arithmetic: 39.4 us -> 28.7 us
    psum x1, blocking collectives: 279 us -> 43.2 us  [per_device(): vectors = lax.psum(gv, ('dp', 'perm', 'blk'))]
    pallas_call x0 -> x1, Pallas kernels: none -> 135 us  [per_device(): pl.pallas_call(functools.partial(layer_kernel, heads), out_shape=(jax.Sha...]
    dot_general x28 -> x0, matrix products: 115 us -> none  [the longest x6 24.6 us: contract_rows(): lax.dot_general(left_rows, right_rows, (((0,), (0,)), ((), ())), preferre...]
    psum x4 -> x1, waiting for transfers between devices: 194 us -> 93.7 us  [per_device(): mine = lax.psum(mine.astype(BF16), 'dp').astype(F32)]
    ppermute x2, waiting for transfers between devices: 0.01 us -> 89.7 us  [the longest x1 78 us: per_device(): mine = mine + lax.ppermute(other, 'perm', [(0, 1), (1, 0)]).astype(F32)]
    unnamed x117 -> x12, local copies, waits for them, and re-layouts: 41.5 us -> 8.38 us
    reduce_sum x13 -> x0, other arithmetic: 24.7 us -> none  [the longest x4 9.79 us: normalize(): centre = values - jnp.mean(values, axis=-1, keepdims=True)]
    all_gather x11 -> x0, blocking collectives: 23.1 us -> none  [the longest x1 2.64 us: per_device(): lax.all_gather(w_out, 'blk', axis=1, tiled=True)]
  transfers between devices with their start and end apart: 14 -> 3, of which waited for: 4 -> 3; matrix products, arithmetic and copies ran while one was open for 14% -> 1% of each run, Pallas kernels for 0% -> 0%
where the time goes in v1:
time: 429 us
  waiting for transfers between devices  183 us (43%)
  Pallas kernels  135 us (31%)
  blocking collectives  43.2 us (10%)
  other arithmetic  28.7 us (7%)
  local copies, waits for them, and re-layouts  23.1 us (5%)
  between operations  14.3 us (3%)
    pallas_call x1, Pallas kernels, per_device(): pl.pallas_call(functools.partial(layer_kernel, heads), out_shape=(jax.Sha...  135 us
    psum x1, waiting for transfers between devices, per_device(): mine = lax.psum(mine.astype(BF16), 'dp').astype(F32)  93.7 us
    ppermute x1, waiting for transfers between devices, per_device(): mine = mine + lax.ppermute(other, 'perm', [(0, 1), (1, 0)]).astype(F32)  78 us
    psum x1, blocking collectives, per_device(): vectors = lax.psum(gv, ('dp', 'perm', 'blk'))  43.2 us
    add x1, other arithmetic, per_device(): gk.astype(F32) + lax.ppermute(gs, 'blk', [(0, 1), (1, 0)]).astype(F32)  12.2 us
    ppermute x1, waiting for transfers between devices, per_device(): lax.ppermute(gs, 'blk', [(0, 1), (1, 0)]).astype(F32)  11.6 us
    convert_element_type x2, other arithmetic, per_device(): mine = lax.psum(mine.astype(BF16), 'dp').astype(F32)  9.66 us
  transfers between devices with their start and end apart: 3, of which 3 were waited for; matrix products, arithmetic and copies ran while one was open for 1% of the time, Pallas kernels for 0%

profile of v1, /device:TPU:0, one launch (start us, length us, event | category | flops | bytes accessed | tf_op | source)
XLA Modules:
  0.0 428.6 jit_solution(16129103053219617488)
XLA Ops:
  8.6 0.7 convert_select_fusion.5
  9.9 0.7 convert_select_fusion.3
  11.3 0.7 convert_select_fusion.1
  13.5 0.8 convert_dynamic-update-slice_fusion
  15.1 1.9 concatenate.3.vec
  17.0 135.2 %layer.1 = (bf16[2,512,768]{2,1,0:T(8,128)(2,1)}, bf16[2,512,768]{2,1,0:T(8,128)(2,1)}, bf16[2,384,4608]{2,1,0:T(8,128)(2,1)}, bf16[2,384,4608]{2,1,0:T(8,128)(2,1)}, f32[16,768]{1,0:T(8,128)}) custom-call(bf16[2,512,768]{2,1,0:T(8,128)(2,1)} %tokens.1, bf16[2,512,768]{2,1,0:T(8,128)(2,1)} %cot.1, s32[2]{0:T(128)} %lengths.1, f32[32,768]{1,0:T(8,128)} %concatenate.3.vec, ...), custom_call_target="tpu_custom_call" | custom-call | tf_op jit(solution)/shard_map/layer/pallas_call | solution.py:462
  152.3 11.6 %collective-permute-done = bf16[2,384,4608]{2,1,0:T(8,128)(2,1)} collective-permute-done((bf16[2,384,4608]{2,1,0:T(8,128)(2,1)}, bf16[2,384,4608]{2,1,0:T(8,128)(2,1)}, u32[]{:S(2)}, u32[]{:S(2)}) %collective-permute-start) | collective-permute-done | bytes 7077920 | tf_op jit(solution)/shard_map/ppermute | solution.py:492
  163.9 12.2 %convert_add_fusion = f32[2,384,4608]{2,1,0:T(8,128)} fusion(bf16[2,384,4608]{2,1,0:T(8,128)(2,1)} %collective-permute-done, bf16[2,384,4608]{2,1,0:T(8,128)(2,1)} %get-tuple-element.24), kind=kLoop, calls=%fused_computation | loop fusion | flops 10616832 | bytes 28311552 | tf_op jit(solution)/shard_map/add | solution.py:492
  176.1 3.4 fusion.1
  179.5 0.7 collective-permute-start.1
  180.2 78.0 %collective-permute-done.1 = bf16[384,4608]{1,0:T(8,128)(2,1)} collective-permute-done((bf16[384,4608]{1,0:T(8,128)(2,1)S(1)}, bf16[384,4608]{1,0:T(8,128)(2,1)}, u32[]{:S(2)}, u32[]{:S(2)}) %collective-permute-start.1) | collective-permute-done | bytes 3538976 | tf_op jit(solution)/shard_map/ppermute | solution.py:495
  258.2 6.8 %fusion = bf16[384,4608]{1,0:T(8,128)(2,1)} fusion(bf16[384,4608]{1,0:T(8,128)(2,1)} %collective-permute-done.1, f32[2,384,4608]{2,1,0:T(8,128)} %convert_add_fusion, s32[]{:T(128)S(6)} %select_n.101), kind=kLoop, calls=%fused_computation.2 | loop fusion | flops 5308416 | bytes 14155780 | tf_op jit(solution)/shard_map/convert_element_type | solution.py:496
  265.1 0.8 copy-done.3
  265.8 43.2 %psum.15 = f32[16,768]{1,0:T(8,128)S(1)} all-reduce(f32[16,768]{1,0:T(8,128)S(1)} %copy-done.3), channel_id=1, replica_groups=mesh['dp'=8,'perm'=2,'blk'=2] {'dp','perm','blk'}, use_global_device_ids=true, to_apply=%region_1.2 | all-reduce | flops 12288 | bytes 98304 | tf_op jit(solution)/shard_map/psum | solution.py:497
  312.2 93.7 %all-reduce.2.cloned.1.call-done = bf16[384,4608]{1,0:T(8,128)(2,1)} async-done(((bf16[384,4608]{1,0:T(8,128)(2,1)}), bf16[384,4608]{1,0:T(8,128)(2,1)}) %all-reduce.2.cloned.1.call-update) | async-done | bytes 3538960 | tf_op jit(solution)/shard_map/psum | solution.py:496
  405.9 2.9 convert_element_type.61
  408.8 0.9 slice_bitcast_fusion.1
  409.6 1.6 slice_bitcast_fusion
  411.2 3.2 copy.37
  414.4 2.1 copy.36
  416.5 1.2 fusion.8
  417.8 1.7 slice.69
  419.5 1.1 copy.52
  420.6 1.1 copy.53
  (50 shorter events, 8.2 us)
Async XLA Ops:
  7.2 398.7 %all-reduce.2.cloned.1.call-start = ((), (), s32[]{:S(2)}) async-start(), calls=%async_computation | async-start | bytes 7077888 | tf_op jit(solution)/shard_map/psum | solution.py:496
  152.2 11.7 %collective-permute-start = (bf16[2,384,4608]{2,1,0:T(8,128)(2,1)}, bf16[2,384,4608]{2,1,0:T(8,128)(2,1)}, u32[]{:S(2)}, u32[]{:S(2)}) collective-permute-start(bf16[2,384,4608]{2,1,0:T(8,128)(2,1)} %get-tuple-element.25), channel_id=1, source_target_pairs={{0,1},{1,0},{2,3},{3,2},{4,5},{5,4},{6,7},{7,6},{8,9},{9,8},{10,11... | collective-permute-start | bytes 21233672 | tf_op jit(solution)/shard_map/ppermute | solution.py:492
  179.5 78.7 %collective-permute-start.1 = (bf16[384,4608]{1,0:T(8,128)(2,1)S(1)}, bf16[384,4608]{1,0:T(8,128)(2,1)}, u32[]{:S(2)}, u32[]{:S(2)}) collective-permute-start(bf16[384,4608]{1,0:T(8,128)(2,1)S(1)} %fusion.1), channel_id=1, source_target_pairs={{0,2},{2,0},{1,3},{3,1},{4,6},{6,4},{5,7},{7,5},{8,10},{10,8},{9,1... | collective-permute-start | bytes 10616840 | tf_op jit(solution)/shard_map/ppermute | solution.py:495
  265.0 0.8 copy-start.3
  411.2 5.3 %copy-start = (bf16[384,4608]{1,0:T(8,128)(2,1)S(1)}, bf16[384,4608]{1,0:T(8,128)(2,1)}, u32[]{:S(2)}) copy-start(bf16[384,4608]{1,0:T(8,128)(2,1)} %all-reduce.2.cloned.1.call-done) | copy-start | bytes 10616836
  416.5 2.9 copy-start.2
  417.8 2.8 copy-start.1
Sparse Core Ops, SparseCore 0:
  265.2 140.6 all-reduce.1
